TPU v7x, 32 devices: a whole 2x2x4 slice. The times are simulated.
32 devices in a mesh: groups: 2 (over y), axial: 8 (over z, x), dp: 2 (over core).
Axes of the slice: x: 2, y: 2, z: 4, core: 2. Of those that a mesh axis runs over, the one named last changes fastest.
Arguments:
- pair: bfloat16 [4, 48, 48, 128], P(('groups', 'dp'), 'axial'), parts along dimension 0, may hold values from -6 to 6
- pair_mask: int32 [4, 48, 48], P(('groups', 'dp'), 'axial'), parts along dimension 0, may hold values from 0 to 1, as said below
- ln_gain: float32 [2, 128], replicated, may hold values from 0.5 to 1.5
- projection_weight: bfloat16 [2, 128, 512], replicated, may hold values from -0.5 to 0.5
- pair_bias_weight: bfloat16 [2, 128, 4], replicated, may hold values from -128 to 128
- w_out: bfloat16 [2, 128, 128], replicated, may hold values from -0.5 to 0.5
- cotangent: bfloat16 [4, 48, 48, 128], P(('groups', 'dp'), None, 'axial'), parts along dimension 0, may hold values from -6 to 6
Outputs:
- pair_out: bfloat16 [4, 48, 48, 128], P(('groups', 'dp'), None, 'axial'), parts along dimension 0
- pair_grad: bfloat16 [4, 48, 48, 128], P(('groups', 'dp'), 'axial'), parts along dimension 0
- grad_ln_gain: float32 [4, 128], P('groups'), parts along dimension 0
- grad_w_proj: float32 [4, 128, 512], P('groups'), parts along dimension 0
- grad_w_bias: float32 [4, 128, 4], P('groups'), parts along dimension 0
- grad_w_out: float32 [4, 128, 128], P('groups'), parts along dimension 0
There are 2 independent parts, one for each index of `groups`. A program takes and returns all parts, laid end to end along the dimension named above; an argument that names none is the same for every part. Nothing has to cross between parts.
Inputs may be any that keep to these rules, and one draw needn't show every extreme that they name: pair_mask[n, i, k] = t[n, i] * t[n, k], where t[n] is 1 on a leading run of the crop's positions and 0 after it; so the mask is symmetric.
All inputs are finite; a program needn't handle non-finite values.
Results may differ from a plain program's by a relative error of at most 0.0095.
The roundings to bfloat16 on the way count: a program that leaves them out, or rounds other values in their place, can miss the bound.
Values may be sent and summed in bfloat16 or wider, within the bound.
A program may use at most 128 MiB of HBM per device.

v0:
```python
import math

import jax
import jax.numpy as jnp
from jax import lax
from jax.sharding import PartitionSpec as P

H = 4


eps = 1e-05
masked = -1000000000.0
highest = lax.Precision.HIGHEST


def layout(column_view, first, second):
    if column_view:
        return "n" + second + first + "c"
    return "n" + first + second + "c"


def apply_layer_norm(pair_input, norm_gain):
    values = pair_input.astype(jnp.float32)
    centered_input = values - jnp.mean(values, axis=-1, keepdims=True)
    spread_values = lax.rsqrt(
        jnp.mean(centered_input * centered_input, axis=-1, keepdims=True) + eps
    )
    standardized_input = centered_input * spread_values
    return (
        standardized_input,
        spread_values,
        (standardized_input * norm_gain).astype(jnp.bfloat16),
    )


def project_input(pair_input, norm_gain, projection_weight, column_view):
    standardized_input, spread_values, normed_input = apply_layer_norm(pair_input, norm_gain)
    proj = jnp.einsum(
        layout(column_view, "a", "b") + ",ce->anbe",
        normed_input,
        projection_weight,
        preferred_element_type=jnp.float32,
    )
    proj = proj.astype(jnp.bfloat16)
    split_heads = proj.reshape(proj.shape[0], proj.shape[1], proj.shape[2], 4, H, -1)
    return (standardized_input, spread_values, normed_input, split_heads)


def local_bias(normed_input, pair_bias_weight, column_view):
    return jnp.einsum(
        layout(column_view, "a", "k") + ",ch->nhak",
        normed_input,
        pair_bias_weight,
        preferred_element_type=jnp.float32,
    )


def row_probs(query, keys, bias_term, keep_row, scale):
    scores = (
        jnp.einsum("nbhd,nkhd->nhbk", query, keys, preferred_element_type=jnp.float32) * scale
        + bias_term
    )
    scores = jnp.where(keep_row[:, None, None, :], scores, masked)
    probs = jax.nn.softmax(scores, axis=-1)
    return (probs, probs.astype(jnp.bfloat16))


def attend_forward(pair_input, keep, params, column_view):
    norm_gain, projection_weight, pair_bias_weight, w_out = params
    standardized_input, spread_values, normed_input, split_heads = project_input(
        pair_input, norm_gain, projection_weight, column_view
    )
    bias_term = lax.all_gather(
        local_bias(normed_input, pair_bias_weight, column_view), "axial", axis=2, tiled=True
    )
    scale = 1.0 / math.sqrt(split_heads.shape[-1])

    def one_row(carry, item):
        query, keys, values, keep_row = item
        probs, probs_b = row_probs(query, keys, bias_term, keep_row, scale)
        return (
            carry,
            jnp.einsum("nhbk,nkhd->nbhd", probs_b, values, preferred_element_type=jnp.float32),
        )

    rows_keep = jnp.moveaxis(keep, 1, 0)
    _, attended = lax.scan(
        one_row,
        jnp.float32(0.0),
        (split_heads[:, :, :, 0], split_heads[:, :, :, 1], split_heads[:, :, :, 2], rows_keep),
    )
    gate = jax.nn.sigmoid(split_heads[:, :, :, 3].astype(jnp.float32))
    gated = (gate * attended).astype(jnp.bfloat16)
    gated = gated.reshape(gated.shape[0], gated.shape[1], gated.shape[2], -1)
    delta = jnp.einsum(
        "anbe,ec->" + layout(column_view, "a", "b"),
        gated,
        w_out,
        preferred_element_type=jnp.float32,
    )
    return ((pair_input.astype(jnp.float32) + delta).astype(jnp.bfloat16), bias_term)


def attend_backward(pair_input, grad_out, keep, params, column_view):
    norm_gain, projection_weight, pair_bias_weight, w_out = params
    standardized_input, spread_values, normed_input, split_heads = project_input(
        pair_input, norm_gain, projection_weight, column_view
    )
    bias_term = lax.all_gather(
        local_bias(normed_input, pair_bias_weight, column_view), "axial", axis=2, tiled=True
    )
    scale = 1.0 / math.sqrt(split_heads.shape[-1])
    store = layout(column_view, "a", "b")
    key_store = layout(column_view, "a", "k")
    d_gated = jnp.einsum(store + ",ec->anbe", grad_out, w_out, preferred_element_type=jnp.float32)
    rows, crops, width = (d_gated.shape[0], d_gated.shape[1], d_gated.shape[2])
    d_gated = d_gated.reshape(rows, crops, width, H, -1)
    gate = jax.nn.sigmoid(split_heads[:, :, :, 3].astype(jnp.float32))

    def one_row(d_bias, item):
        query, keys, values, keep_row, gate_row, d_row = item
        probs, probs_b = row_probs(query, keys, bias_term, keep_row, scale)
        attended = jnp.einsum(
            "nhbk,nkhd->nbhd", probs_b, values, preferred_element_type=jnp.float32
        )
        gated = (gate_row * attended).astype(jnp.bfloat16)
        d_att = (d_row * gate_row).astype(jnp.bfloat16)
        d_gate = (d_row * attended * gate_row * (1.0 - gate_row)).astype(jnp.bfloat16)
        d_probs = jnp.einsum("nbhd,nkhd->nhbk", d_att, values, preferred_element_type=jnp.float32)
        total = jnp.sum(probs * d_probs, axis=-1, keepdims=True)
        d_scores = jnp.where(keep_row[:, None, None, :], probs * (d_probs - total), 0.0)
        d_scores_b = d_scores.astype(jnp.bfloat16)
        d_query = (
            jnp.einsum("nhbk,nkhd->nbhd", d_scores_b, keys, preferred_element_type=jnp.float32)
            * scale
        ).astype(jnp.bfloat16)
        d_keys = (
            jnp.einsum("nhbk,nbhd->nkhd", d_scores_b, query, preferred_element_type=jnp.float32)
            * scale
        ).astype(jnp.bfloat16)
        d_values = jnp.einsum(
            "nhbk,nbhd->nkhd", probs_b, d_att, preferred_element_type=jnp.float32
        ).astype(jnp.bfloat16)
        d_split = jnp.stack([d_query, d_keys, d_values, d_gate], axis=2)
        return (d_bias + d_scores, (d_split, gated))

    rows_keep = jnp.moveaxis(keep, 1, 0)
    items = (
        split_heads[:, :, :, 0],
        split_heads[:, :, :, 1],
        split_heads[:, :, :, 2],
        rows_keep,
        gate,
        d_gated,
    )
    d_bias, (d_split, gated) = lax.scan(one_row, jnp.zeros(bias_term.shape, jnp.float32), items)
    d_proj = d_split.reshape(rows, crops, width, -1)
    gated = gated.reshape(rows, crops, width, -1)
    own_bias = lax.psum_scatter(d_bias, "axial", scatter_dimension=2, tiled=True)
    grad_w_out = jnp.einsum(
        "anbe," + store + "->ec", gated, grad_out, preferred_element_type=jnp.float32
    )
    layer_norm_gradient = jnp.einsum(
        "anbe,ce->" + store, d_proj, projection_weight, preferred_element_type=jnp.float32
    )
    layer_norm_gradient = layer_norm_gradient + jnp.einsum(
        "nhak,ch->" + key_store, own_bias, pair_bias_weight.astype(jnp.float32), precision=highest
    )
    grad_w_proj = jnp.einsum(
        store + ",anbe->ce", normed_input, d_proj, preferred_element_type=jnp.float32
    )
    grad_w_bias = jnp.einsum(
        key_store + ",nhak->ch", normed_input.astype(jnp.float32), own_bias, precision=highest
    )
    normalized_gradient = layer_norm_gradient * norm_gain
    gain_gradient = jnp.sum(layer_norm_gradient * standardized_input, axis=(0, 1, 2))
    inner_product = (
        normalized_gradient
        - jnp.mean(normalized_gradient, axis=-1, keepdims=True)
        - standardized_input
        * jnp.mean(normalized_gradient * standardized_input, axis=-1, keepdims=True)
    )
    d_in = (grad_out.astype(jnp.float32) + spread_values * inner_product).astype(jnp.bfloat16)
    return (d_in, (gain_gradient, grad_w_proj, grad_w_bias, grad_w_out))


def local(pair, pair_mask, ln_gain, projection_weight, pair_bias_weight, w_out, cotangent):
    keep = pair_mask > 0
    first = (ln_gain[0], projection_weight[0], pair_bias_weight[0], w_out[0])
    second = (ln_gain[1], projection_weight[1], pair_bias_weight[1], w_out[1])
    middle, first_bias = attend_forward(pair, keep, first, False)
    columns = lax.all_to_all(middle, "axial", split_axis=2, concat_axis=1, tiled=True)
    pair_out, second_bias = attend_forward(columns, keep, second, True)
    d_columns, grads_second = attend_backward(columns, cotangent, keep, second, True)
    d_middle = lax.all_to_all(d_columns, "axial", split_axis=1, concat_axis=2, tiled=True)
    pair_grad, grads_first = attend_backward(pair, d_middle, keep, first, False)
    summed = lax.psum(
        (
            grads_first[0],
            grads_first[1],
            grads_first[2],
            grads_first[3],
            grads_second[0],
            grads_second[1],
            grads_second[2],
            grads_second[3],
        ),
        ("axial", "dp"),
    )
    grads_first = tuple(summed[:4])
    grads_second = tuple(summed[4:])
    stacked = [jnp.stack([grads_first[idx], grads_second[idx]]) for idx in range(4)]
    return (pair_out, pair_grad, stacked[0], stacked[1], stacked[2], stacked[3])


def solution(mesh):
    placed = (
        P(("groups", "dp"), "axial", None, None),
        P(("groups", "dp"), "axial", None),
        P(),
        P(),
        P(),
        P(),
        P(("groups", "dp"), None, "axial", None),
    )
    return jax.shard_map(
        local,
        mesh=mesh,
        in_specs=placed,
        out_specs=(
            P(("groups", "dp"), None, "axial", None),
            P(("groups", "dp"), "axial", None, None),
            P("groups", None),
            P("groups", None, None),
            P("groups", None, None),
            P("groups", None, None),
        ),
        check_vma=False,
    )
```

profile of v0, /device:TPU:0, one launch (start us, length us, event | category | flops | bytes accessed | tf_op | source)
XLA Modules:
  0.0 403.1 jit_solution(8443408198221416750)
XLA Ops:
  8.7 1.0 convert_reduce_fusion
  10.6 32.3 %all-gather = f32[4,48,48]{2,0,1:T(4,128)S(1)} all-gather(f32[4,6,48]{2,0,1:T(4,128)S(1)} %convolution_bitcast_fusion.16), channel_id=2, replica_groups=mesh['groups'=2,'axial'=8,'dp'=2] {'axial'}, dimensions={1}, use_global_device_ids=true | all-gather | bytes 41472 | tf_op jit(solution)/shard_map/all_gather | solution.py:73
  43.9 3.8 while.50
  50.1 5.6 %all-to-all-start = ((bf16[1,6,48,128]{3,1,0,2:T(8,128)(2,1)}), bf16[1,6,48,128]{3,1,0,2:T(8,128)(2,1)S(1)}, u32[]{:S(2)}, u32[]{:S(2)}) async-start(bf16[1,6,48,128]{3,1,0,2:T(8,128)(2,1)} %copy.340), calls=%async_computation | async-start | bytes 196608 | tf_op jit(solution)/shard_map/all_to_all | solution.py:192
  58.0 4.7 %all-to-all-done = bf16[1,6,48,128]{3,1,0,2:T(8,128)(2,1)S(1)} async-done(((bf16[1,6,48,128]{3,1,0,2:T(8,128)(2,1)}), bf16[1,6,48,128]{3,1,0,2:T(8,128)(2,1)S(1)}, u32[]{:S(2)}, u32[]{:S(2)}) %all-to-all-start) | async-done | bytes 73760 | tf_op jit(solution)/shard_map/all_to_all | solution.py:192
  66.8 30.5 %all_gather.9 = f32[1,4,48,48]{3,1,0,2:T(4,128)S(1)} all-gather(f32[1,4,6,48]{3,1,0,2:T(4,128)S(1)} %convolution_bitcast_fusion.15), channel_id=1, replica_groups=mesh['groups'=2,'axial'=8,'dp'=2] {'axial'}, dimensions={2}, use_global_device_ids=true | all-gather | bytes 41472 | tf_op jit(solution)/shard_map/all_gather | solution.py:73
  98.3 15.9 %while.51 = (s32[]{:T(128)}, f32[6,1,48,4,32]{2,4,3,1,0:T(8,128)}, bf16[6,1,48,4,32]{2,4,3,1,0:T(8,128)(2,1)}, pred[6,1,48]{2,1,0:T(4,128)(4,1)}, bf16[6,1,48,4,...) while((s32[]{:T(128)}, f32[6,1,48,4,32]{2,4,3,1,0:T(8,128)}, ...), condition=%wide.region_11.12_spmd, body=%wide.region_8.11_spmd.sunk | while | flops 1871136 | bytes 666561 | solution.py:87
  99.4 1.5 fusion.321
  102.0 1.5 fusion.321
  104.7 1.5 fusion.321
  107.3 1.5 fusion.321
  110.0 1.5 fusion.321
  112.6 1.5 fusion.321
  114.2 1.8 fusion.148
  116.9 45.1 %while.52 = (s32[]{:T(128)}, f32[1,4,48,48]{2,3,1,0:T(8,128)}, bf16[6,1,48,4,4,32]{2,5,4,3,1,0:T(8,128)(2,1)S(1)}, bf16[6,1,48,4,32]{2,4,3,1,0:T(8,128)(2,1)}, p...) while((s32[]{:T(128)}, f32[1,4,48,48]{2,3,1,0:T(8,128)}, ...), condition=%wide.region_16.17_spmd.clone, body=%wide.region_12.16_spmd.clone.sunk | while | flops 3987745 | bytes 1563291 | solution.py:156
  116.9 1.1 fusion.334
  118.0 1.0 fusion.333
  119.0 1.5 fusion.335
  122.8 1.5 fusion.336
  124.4 1.2 fusion.334
  125.5 1.0 fusion.333
  126.5 1.5 fusion.335
  130.3 1.5 fusion.336
  131.9 1.2 fusion.334
  133.1 1.0 fusion.333
  134.0 1.5 fusion.335
  137.8 1.5 fusion.336
  139.4 1.1 fusion.334
  140.6 1.0 fusion.333
  141.5 1.5 fusion.335
  145.3 1.5 fusion.336
  146.9 1.2 fusion.334
  148.1 1.0 fusion.333
  149.1 1.5 fusion.335
  152.9 1.5 fusion.336
  154.5 1.1 fusion.334
  155.6 1.0 fusion.333
  156.6 1.5 fusion.335
  160.3 1.5 fusion.336
  161.9 1.9 convolution_bitcast_fusion.13
  163.9 34.8 %all-reduce = f32[1,4,48,48]{3,1,0,2:T(4,128)S(1)} all-reduce(f32[1,4,48,48]{3,1,0,2:T(4,128)S(1)} %copy.365), channel_id=3, replica_groups=mesh['groups'=2,'axial'=8,'dp'=2] {'axial'}, use_global_device_ids=true, to_apply=%region_17.18.clone | all-reduce | flops 9216 | bytes 73728
  200.5 1.3 convolution_bitcast_fusion.4
  203.6 3.4 all-to-all-start.1
  207.3 6.7 %all-to-all-done.1 = bf16[1,48,6,128]{3,2,0,1:T(8,128)(2,1)S(1)} async-done(((bf16[1,48,6,128]{3,2,0,1:T(8,128)(2,1)}), bf16[1,48,6,128]{3,2,0,1:T(8,128)(2,1)S(1)}, u32[]{:S(2)}, u32[]{:S(2)}) %all-to-all-start.1) | async-done | bytes 73760 | tf_op jit(solution)/shard_map/all_to_all | solution.py:195
  215.4 20.5 %while.53 = (s32[]{:T(128)}, f32[1,4,48,48]{2,3,1,0:T(8,128)S(1)}, bf16[6,1,48,4,4,32]{2,5,4,3,1,0:T(8,128)(2,1)S(1)}, bf16[6,1,48,4,32]{2,4,3,1,0:T(8,128)(2,1)...) while((s32[]{:T(128)}, f32[1,4,48,48]{2,3,1,0:T(8,128)S(1)}, ...), condition=%wide.region_24.25_spmd.clone, body=%wide.region_20.24_spmd.clone.sunk | while | flops 3987745 | bytes 1410107 | solution.py:156
  216.0 1.0 fusion.353
  217.8 0.9 fusion.356
  219.5 1.0 fusion.353
  221.2 0.9 fusion.356
  222.9 1.0 fusion.353
  224.6 0.9 fusion.356
  226.3 1.0 fusion.353
  228.1 0.9 fusion.356
  229.8 1.0 fusion.353
  231.5 0.9 fusion.356
  233.2 1.0 fusion.353
  234.9 0.9 fusion.356
  236.6 1.3 convolution_bitcast_fusion.5
  237.9 0.9 convolution_bitcast_fusion.14
  238.8 34.6 %all-reduce.1 = f32[1,4,48,48]{3,1,0,2:T(4,128)S(1)} all-reduce(f32[1,4,48,48]{3,1,0,2:T(4,128)S(1)} %copy.382), channel_id=4, replica_groups=mesh['groups'=2,'axial'=8,'dp'=2] {'axial'}, use_global_device_ids=true, to_apply=%region_25.26.clone | all-reduce | flops 9216 | bytes 73728
  274.2 30.0 %all-reduce.2 = (f32[1,128]{1,0:T(1,128)S(1)}, f32[1,128]{1,0:T(1,128)S(1)}, f32[1,128,4]{1,2,0:T(4,128)S(1)}, f32[1,128,4]{1,2,0:T(4,128)S(1)}) all-reduce(f32[1,128]{1,0:T(1,128)S(1)} %bitcast.692, f32[1,128]{1,0:T(1,128)S(1)} %bitcast.693, ...), channel_id=1, replica_groups=mesh['groups'=2,'axial'=8,'dp'=2] {'axial','dp'}, use_global_device_ids=true, to_apply=%region_31.32 | all-reduce | flops 1280 | bytes 10240 | tf_op jit(solution)/shard_map/psum | solution.py:197
  305.4 0.9 fusion.163
  306.3 87.4 %all-reduce.6.cloned.1.call-done = (f32[1,128,512]{2,1,0:T(8,128)}, f32[1,128,512]{2,1,0:T(8,128)}, f32[1,128,128]{2,1,0:T(8,128)}, f32[1,128,128]{2,1,0:T(8,128)}) async-done(((f32[1,128,512]{2,1,0:T(8,128)}, f32[1,128,512]{2,1,0:T(8,128)}, f32[1,128,128]{2,1,0:T(8,128)}, f32[1,128,128]{2,1,0:T(8,128)}), (f32[1,128,512]{2,1,0:T(8,128)}, f32[1,128,512]{2,1,0:T(8,128)}, f32[1,128,128]{2,1,0:T(8,128)}, ...) | async-done | bytes 655376 | tf_op jit(solution)/shard_map/psum | solution.py:197
  393.7 1.9 pad_maximum_fusion
  (306 shorter events, 54.9 us)
Async XLA Ops:
  7.2 2.5 copy-start
  8.7 34.4 %copy-start.22 = (f32[128]{0:T(128)}, f32[128]{0:T(128)S(1)}, u32[]{:S(2)}) copy-start(f32[128]{0:T(128)S(1)} %get-tuple-element.598) | copy-start | bytes 1540
  8.7 55.0 %copy-start.19 = (f32[128]{0:T(128)}, f32[128]{0:T(128)S(1)}, u32[]{:S(2)}) copy-start(f32[128]{0:T(128)S(1)} %get-tuple-element.599) | copy-start | bytes 1540
  9.7 0.7 copy-start.24
  9.9 33.2 %copy-start.1 = (bf16[2,128,512]{2,1,0:T(8,128)(2,1)S(1)}, bf16[2,128,512]{2,1,0:T(8,128)(2,1)}, u32[]{:S(2)}) copy-start(bf16[2,128,512]{2,1,0:T(8,128)(2,1)} %param.18) | copy-start | bytes 786436
  47.7 0.7 copy-start.7
  48.3 0.6 copy-start.26
  48.3 0.8 copy-start.8
  50.1 5.6 %copy-start.5 = (bf16[1,48,6,128]{3,1,2,0:T(8,128)(2,1)S(1)}, bf16[1,48,6,128]{3,1,2,0:T(8,128)(2,1)}, u32[]{:S(2)}) copy-start(bf16[1,48,6,128]{3,1,2,0:T(8,128)(2,1)} %param.21) | copy-start | bytes 221188
  50.1 12.7 %all-to-all-start = ((bf16[1,6,48,128]{3,1,0,2:T(8,128)(2,1)}), bf16[1,6,48,128]{3,1,0,2:T(8,128)(2,1)S(1)}, u32[]{:S(2)}, u32[]{:S(2)}) async-start(bf16[1,6,48,128]{3,1,0,2:T(8,128)(2,1)} %copy.340), calls=%async_computation | async-start | bytes 196608 | tf_op jit(solution)/shard_map/all_to_all | solution.py:192
  56.0 0.7 copy-start.27
  120.5 0.7 copy-start.18
  121.2 0.9 copy-start.13
  121.2 0.9 copy-start.21
  122.1 0.6 copy-start.14
  128.0 0.7 copy-start.18
  128.7 0.9 copy-start.13
  128.7 0.9 copy-start.21
  129.7 0.6 copy-start.14
  135.5 0.7 copy-start.18
  136.2 0.9 copy-start.13
  136.2 0.9 copy-start.21
  137.2 0.6 copy-start.14
  143.0 0.7 copy-start.18
  143.7 0.9 copy-start.13
  143.7 0.9 copy-start.21
  144.7 0.6 copy-start.14
  150.6 0.7 copy-start.18
  151.3 0.9 copy-start.13
  151.3 0.9 copy-start.21
  152.2 0.6 copy-start.14
  158.0 0.7 copy-start.18
  158.7 0.9 copy-start.13
  158.7 0.9 copy-start.21
  159.7 0.6 copy-start.14
  161.9 1.9 copy-start.15
  163.8 34.9 %copy-start.2 = (bf16[2,128,512]{2,1,0:T(8,128)(2,1)S(1)}, bf16[2,128,512]{2,1,0:T(8,128)(2,1)}, u32[]{:S(2)}) copy-start(bf16[2,128,512]{2,1,0:T(8,128)(2,1)} %param.18) | copy-start | bytes 786436
  198.7 0.9 copy-start.4
  198.7 0.9 copy-start.9
  199.6 0.9 copy-start.10
  199.6 0.9 copy-start.11
  199.6 0.9 copy-start.20
  200.5 1.3 copy-start.25
  201.8 0.9 copy-start.6
  203.6 10.4 %all-to-all-start.1 = ((bf16[1,48,6,128]{3,2,0,1:T(8,128)(2,1)}), bf16[1,48,6,128]{3,2,0,1:T(8,128)(2,1)S(1)}, u32[]{:S(2)}, u32[]{:S(2)}) async-start(bf16[1,48,6,128]{3,2,0,1:T(8,128)(2,1)} %copy.368), calls=%async_computation.1 | async-start | bytes 196608 | tf_op jit(solution)/shard_map/all_to_all | solution.py:195
  206.9 186.7 %all-reduce.6.cloned.1.call-start = ((), (), s32[]{:S(2)}) async-start(), calls=%async_computation.2 | async-start | bytes 1310720 | tf_op jit(solution)/shard_map/psum | solution.py:197
  214.5 0.9 copy-start.12
  215.4 20.5 %copy-start.3 = (bf16[2,128,512]{2,1,0:T(8,128)(2,1)S(1)}, bf16[2,128,512]{2,1,0:T(8,128)(2,1)}, u32[]{:S(2)}) copy-start(bf16[2,128,512]{2,1,0:T(8,128)(2,1)} %param.18) | copy-start | bytes 786436
  235.9 0.7 copy-start.23
  393.7 1.9 copy-start.16
  393.7 1.9 copy-start.17
Sparse Core Ops, SparseCore 0:
  304.9 88.6 all-reduce.5
where the time goes:
time: 406 us; the launch traced here: 403 us
  blocking collectives  162 us (40%)
  waiting for transfers between devices  98.9 us (24%)
  matrix products  67 us (17%)
  local copies, waits for them, and re-layouts  38.5 us (9%)
  between operations  15.2 us (4%)
  other arithmetic  11.4 us (3%)
  starting transfers between devices  9 us (2%)
    psum x1, waiting for transfers between devices, local(): lax.psum((grads_first[0], grads_first[1], grads_first[2], grads_first[3],...  87.4 us
    unnamed x2, blocking collectives  69.4 us
    all_gather x2, blocking collectives, attend_forward(): lax.all_gather(local_bias(normed_input, pair_bias_weight, column_view), '...  62.9 us
    psum x1, blocking collectives, local(): lax.psum((grads_first[0], grads_first[1], grads_first[2], grads_first[3],...  30 us
    dot_general x24, matrix products, one_row(): jnp.einsum('nhbk,nkhd->nbhd', probs_b, values, preferred_element_type=jnp...  24.8 us
    sub x24, matrix products, row_probs(): probs = jax.nn.softmax(scores, axis=-1)  13.4 us
    dot_general x12, matrix products, one_row(): jnp.einsum('nbhd,nkhd->nhbk', d_att, values, preferred_element_type=jnp.f...  11.5 us
    broadcast_in_dim x12, local copies, waits for them, and re-layouts, one_row(): jnp.where(keep_row[:, None, None, :], probs * (d_probs - total), 0.0)  10.8 us
  transfers between devices with their start and end apart: 3, of which 3 were waited for; matrix products, arithmetic and copies ran while one was open for 1% of the time, Pallas kernels for 0%

commit v1 on v0

v1 whole, which is shorter than its diff:
```python
import functools
import math

import jax
import jax.numpy as jnp
from jax import lax
from jax.experimental import pallas as pl
from jax.experimental.pallas import tpu as pltpu
from jax.sharding import PartitionSpec as P

MESH = pl.DeviceIdType.MESH
F32, BF16 = jnp.float32, jnp.bfloat16
H = 4
EPS = 1e-05
MASKED = -1000000000.0
HIGHEST = lax.Precision.HIGHEST


def dot(a, b, ca, cb, precision=None):
    return lax.dot_general(a, b, (((ca,), (cb,)), ((), ())), precision=precision, preferred_element_type=F32)


def kernel(
    n, rows, width, small, block, chunk,
    pair_ref, mask_ref, gain_ref, wproj_ref, wbias_ref, wout_ref, cot_ref, spread_ref, gather_ref,
    out_ref, grad_ref, gproj_ref, gout_ref, tail_ref,
    xhat, rstd, normed, proj, gate, att, dgated, gated, dproj, x2, dy1, bias, dacc, kept,
    bgat, dsend, drecv, asend, arecv, part, fromcore, half, red, full, tails,
    send_sem, recv_sem, core_send, core_recv,
):
    me = lax.axis_index("axial")
    core = lax.axis_index("dp")
    other = 1 - core
    channels = pair_ref.shape[1]
    head = channels // H
    scale = 1.0 / math.sqrt(head)
    stack = H if small else 1
    half_rows = n * chunk

    def slot_of(l):
        return l if small else 0

    def steps(low, high, body):
        if small:
            for idx in range(low, high):
                body(idx)
        else:
            lax.fori_loop(low, high, lambda idx, c: (body(idx), c)[1], 0)

    barrier = pltpu.get_barrier_semaphore()

    def greet(off):
        pl.semaphore_signal(barrier, inc=1, device_id={"axial": lax.rem(me + off, n)}, device_id_type=MESH)

    steps(1, n, greet)
    pl.semaphore_signal(barrier, inc=1, device_id={"dp": other}, device_id_type=MESH)

    def axial_copy(phase, off, source, target, slot):
        peer = lax.rem(me + off, n)
        return pltpu.make_async_remote_copy(
            src_ref=source(peer), dst_ref=target(slot),
            send_sem=send_sem.at[phase, off], recv_sem=recv_sem.at[phase, off],
            device_id={"axial": peer}, device_id_type=MESH,
        )

    def start(phase, source, target):
        steps(1, n, lambda off: axial_copy(phase, off, source, target, me).start())

    def finish(phase, source, target):
        steps(1, n, lambda off: axial_copy(phase, off, source, target, lax.rem(me + n - off, n)).wait())

    def core_copy(phase, source, target):
        return pltpu.make_async_remote_copy(
            src_ref=source, dst_ref=target, send_sem=core_send.at[phase], recv_sem=core_recv.at[phase],
            device_id={"dp": other}, device_id_type=MESH,
        )

    def at_row(a):
        return pl.ds(a * width if small else pl.multiple_of(a * width, 16), width)

    lanes = lax.broadcasted_iota(jnp.int32, (1, channels), 1)
    head_masks = [jnp.where((lanes >= h * head) & (lanes < (h + 1) * head), 1.0, 0.0) for h in range(H)]

    def stacked(value, first):
        value = value.astype(F32)
        return jnp.concatenate([value * head_masks[first + h] for h in range(stack)], axis=0).astype(BF16)

    def merged(value, first):
        total = value[:width] * head_masks[first]
        for h in range(1, stack):
            total = total + value[h * width : (h + 1) * width] * head_masks[first + h]
        return total

    def prepare(l, x_ref):
        x = x_ref[...].astype(F32)
        centered = x - jnp.mean(x, axis=-1, keepdims=True)
        spread = lax.rsqrt(jnp.mean(centered * centered, axis=-1, keepdims=True) + EPS)
        hat = centered * spread
        xhat[l] = hat
        rstd[l] = jnp.broadcast_to(spread, hat.shape)
        normed[l] = (hat * gain_ref[l : l + 1]).astype(BF16)

        def own_bias(a):
            bgat[slot_of(l), me * rows + a] = dot(wbias_ref[l], normed[l, at_row(a)], 1, 1)

        steps(0, rows, own_bias)

    def project(l):
        values = dot(normed[l], wproj_ref[l], 1, 0).astype(BF16)
        proj[l] = values
        gate[l] = jax.nn.sigmoid(values[:, 3 * channels :].astype(F32))

    def bias_source(l):
        return lambda peer: bgat.at[slot_of(l), pl.ds(me * rows, rows)]

    def bias_target(l):
        return lambda slot: bgat.at[slot_of(l), pl.ds(slot * rows, rows)]

    def stack_bias(l):
        for h in range(H):
            bias[l, h * width : (h + 1) * width] = bgat[slot_of(l), :, h, :]

    def probabilities(l, a, first, queries, keys):
        scores = dot(queries, keys, 1, 1) * scale + bias[l, first * width : (first + stack) * width]
        scores = jnp.where(mask_ref[pl.ds(a, 1)] > 0, scores, MASKED)
        top = jnp.max(scores, axis=-1, keepdims=True)
        weights = jnp.exp(scores - top)
        return weights * (1.0 / jnp.sum(weights, axis=-1, keepdims=True))

    def column(l, a, part_index):
        return proj[l, at_row(a), part_index * channels : (part_index + 1) * channels]

    def forward_row(a):
        keys, values, query = column(0, a, 1), column(0, a, 2), column(0, a, 0)
        total = None
        for first in range(0, H, stack):
            probs = probabilities(0, a, first, stacked(query, first), keys)
            if small:
                kept[a] = probs
            term = merged(dot(probs.astype(BF16), values, 1, 0), first)
            total = term if total is None else total + term
        att[0, at_row(a)] = total

    def backward_row(l, a):
        keys, values, query = column(l, a, 1), column(l, a, 2), column(l, a, 0)
        gates = gate[l, at_row(a)]
        d_row = dgated[at_row(a)]
        d_att = (d_row * gates).astype(BF16)
        keep = mask_ref[pl.ds(a, 1)] > 0
        total = d_query = d_keys = d_values = None
        for first in range(0, H, stack):
            queries = stacked(query, first)
            probs = kept[a] if small and l == 0 else probabilities(l, a, first, queries, keys)
            probs_b = probs.astype(BF16)
            d_stack = stacked(d_att, first)
            if l == 1:
                term = merged(dot(probs_b, values, 1, 0), first)
                total = term if total is None else total + term
            d_probs = dot(d_stack, values, 1, 1)
            inner = jnp.sum(probs * d_probs, axis=-1, keepdims=True)
            d_scores = jnp.where(keep, probs * (d_probs - inner), 0.0)
            where = slice(first * width, (first + stack) * width)
            if small and a == 0:
                dacc[where] = d_scores
            else:
                dacc[where] += d_scores
            d_b = d_scores.astype(BF16)
            terms = (merged(dot(d_b, keys, 1, 0), first), dot(d_b, queries, 0, 0), dot(probs_b, d_stack, 0, 0))
            if d_query is None:
                d_query, d_keys, d_values = terms
            else:
                d_query, d_keys, d_values = d_query + terms[0], d_keys + terms[1], d_values + terms[2]
        if l == 1:
            att[1, at_row(a)] = total
        else:
            total = att[0, at_row(a)]
        d_gate = d_row * total * gates * (1.0 - gates)
        dproj[at_row(a), :channels] = (d_query * scale).astype(BF16)
        dproj[at_row(a), channels : 2 * channels] = (d_keys * scale).astype(BF16)
        dproj[at_row(a), 2 * channels : 3 * channels] = d_values.astype(BF16)
        dproj[at_row(a), 3 * channels :] = d_gate.astype(BF16)

    def gate_output(l, x_ref):
        values = (gate[l] * att[l]).astype(BF16)
        gated[l] = values
        return (x_ref[...].astype(F32) + dot(values, wout_ref[l], 1, 0)).astype(BF16)

    def turn_send(index, value_at):
        def turned(base, length):
            total = None
            for a in range(rows):
                spots = lax.broadcasted_iota(jnp.int32, (length, width), 0) + (base - a)
                chosen = jnp.where(spots == spread_ref[...], 1.0, 0.0).astype(BF16)
                term = dot(chosen, value_at(a), 1, 0)
                total = term if total is None else total + term
            return total.astype(BF16)

        def one(peer):
            asend[slot_of(index), peer] = turned(peer * block, block)

        if small:
            asend[index] = turned(0, n * block).reshape(n, block, channels)
        else:
            steps(0, n, one)
        arecv[slot_of(index), me] = asend[slot_of(index), me]
        start(4 + index, lambda peer: asend.at[slot_of(index), peer], lambda slot: arecv.at[slot_of(index), slot])

    def turn_receive(index, target):
        finish(4 + index, lambda peer: asend.at[slot_of(index), peer], lambda slot: arecv.at[slot_of(index), slot])
        arrived = arecv[slot_of(index)].reshape(n * block, channels)

        def one(a):
            spots = lax.broadcasted_iota(jnp.int32, (width, n * block), 1) - a * rows
            chosen = jnp.where(spots == gather_ref[...], 1.0, 0.0).astype(BF16)
            target[at_row(a)] = dot(chosen, arrived, 1, 0).astype(BF16)

        steps(0, rows, one)

    def ds_source(l):
        return lambda peer: dsend.at[slot_of(l), pl.ds(peer * rows, rows)]

    def ds_target(l):
        return lambda slot: drecv.at[slot_of(l), slot]

    def send_bias_grad(l):
        for h in range(H):
            dsend[slot_of(l), :, h, :] = dacc[h * width : (h + 1) * width]
        drecv[slot_of(l), me] = dsend[slot_of(l), pl.ds(me * rows, rows)]
        start(2 + l, ds_source(l), ds_target(l))

    def weight_grads(l, dy):
        values = dot(normed[l], dproj[...], 0, 0)
        for e in range(4):
            part[l, e * channels : (e + 1) * channels] = values[:, e * channels : (e + 1) * channels]
        part[l, 4 * channels : 5 * channels] = dot(gated[l], dy, 0, 0)

    def core_first(l):
        return core_copy(l, part.at[l, pl.ds(other * half_rows, half_rows)], fromcore.at[l])

    def reduce_source(l):
        return lambda peer: half.at[l, peer]

    def reduce_target(l):
        return lambda slot: red.at[l, slot]

    def core_sum(l):
        core_first(l).wait()
        value = part[l, pl.ds(pl.multiple_of(core * half_rows, 8), half_rows)] + fromcore[l]
        half[l] = value.reshape(n, chunk, channels)
        red[l, me] = half[l, me]
        start(6 + l, reduce_source(l), reduce_target(l))

    def full_source(l):
        return lambda peer: full.at[l, core, me]

    def full_target(l):
        return lambda slot: full.at[l, core, slot]

    def axial_sum(l):
        finish(6 + l, reduce_source(l), reduce_target(l))
        full[l, core, me] = jnp.sum(red[l], axis=0)
        start(8 + l, full_source(l), full_target(l))

    def core_last(l):
        return core_copy(2 + l, full.at[l, core], full.at[l, core])

    def core_last_wait(l):
        return core_copy(2 + l, full.at[l, core], full.at[l, other])

    def layer_norm_grad(l, dn, dy):
        finish(2 + l, ds_source(l), ds_target(l))
        own = jnp.sum(drecv[slot_of(l)], axis=0)
        extra, bias_grad = [], None
        weights = wbias_ref[l].astype(F32)
        for a in range(rows):
            extra.append(dot(own[a], weights, 0, 0, HIGHEST))
            term = dot(own[a], normed[l, a * width : (a + 1) * width].astype(F32), 1, 0, HIGHEST)
            bias_grad = term if bias_grad is None else bias_grad + term
        dn = dn + jnp.concatenate(extra, axis=0)
        hat = xhat[l]
        gain_grad = jnp.sum(dn * hat, axis=0, keepdims=True)
        d_hat = dn * gain_ref[l : l + 1]
        inner = (
            d_hat
            - jnp.mean(d_hat, axis=-1, keepdims=True)
            - hat * jnp.mean(d_hat * hat, axis=-1, keepdims=True)
        )
        tails[me, l * 16 : l * 16 + 8] = bias_grad
        tails[me, l * 16 + 8 : l * 16 + 16] = jnp.broadcast_to(gain_grad, (8, channels))
        return (dy.astype(F32) + rstd[l] * inner).astype(BF16)

    dsend[...] = jnp.zeros(dsend.shape, F32)
    if half_rows * 2 > 5 * channels:
        part[...] = jnp.zeros(part.shape, F32)

    prepare(0, pair_ref)
    pl.semaphore_wait(barrier, n)
    start(0, bias_source(0), bias_target(0))
    project(0)
    finish(0, bias_source(0), bias_target(0))
    stack_bias(0)
    steps(0, rows, forward_row)
    asend_value = gate_output(0, pair_ref)
    turn_send(0, lambda a: asend_value[a * width : (a + 1) * width])
    dgated[...] = dot(cot_ref[...], wout_ref[1], 1, 1)
    turn_receive(0, x2)

    prepare(1, x2)
    start(1, bias_source(1), bias_target(1))
    project(1)
    finish(1, bias_source(1), bias_target(1))
    stack_bias(1)
    if not small:
        dacc[...] = jnp.zeros(dacc.shape, F32)
    steps(0, rows, functools.partial(backward_row, 1))
    send_bias_grad(1)
    out_ref[...] = gate_output(1, x2)
    dn = dot(dproj[...], wproj_ref[1], 1, 1)
    weight_grads(1, cot_ref[...])
    core_first(1).start()
    d_columns = layer_norm_grad(1, dn, cot_ref[...])
    turn_send(1, lambda a: d_columns[a * width : (a + 1) * width])
    core_sum(1)
    turn_receive(1, dy1)

    dgated[...] = dot(dy1[...], wout_ref[0], 1, 1)
    if not small:
        dacc[...] = jnp.zeros(dacc.shape, F32)
    steps(0, rows, functools.partial(backward_row, 0))
    send_bias_grad(0)
    axial_sum(1)
    weight_grads(0, dy1[...])
    core_first(0).start()
    dn = dot(dproj[...], wproj_ref[0], 1, 1)
    core_sum(0)
    grad_ref[...] = layer_norm_grad(0, dn, dy1[...])
    start(10, lambda peer: tails.at[me], lambda slot: tails.at[slot])
    axial_sum(0)
    finish(8 + 1, full_source(1), full_target(1))
    core_last(1).start()
    finish(10, lambda peer: tails.at[me], lambda slot: tails.at[slot])
    mine = jnp.sum(tails[...], axis=0)
    tail_ref[0] = mine
    core_copy(4, tail_ref.at[0], tail_ref.at[1]).start()
    finish(8, full_source(0), full_target(0))
    core_last(0).start()
    core_copy(4, tail_ref.at[0], tail_ref.at[1]).wait()
    tail_ref[0] = tail_ref[0] + tail_ref[1]
    for l in (1, 0):
        core_last_wait(l).wait()
        values = full[l].reshape(2 * half_rows, channels)
        for e in range(4):
            gproj_ref[l, :, e * channels : (e + 1) * channels] = values[e * channels : (e + 1) * channels]
        gout_ref[l] = values[4 * channels : 5 * channels]


def local(n, pair, pair_mask, ln_gain, projection_weight, pair_bias_weight, w_out, cotangent):
    rows, width, channels = pair.shape[1:]
    small = width <= 128
    slots = 2 if small else 1
    block = -(-rows * rows // 16) * 16
    chunk = -(-5 * channels // (2 * n * 8)) * 8
    wbias = jnp.pad(jnp.swapaxes(pair_bias_weight, 1, 2), ((0, 0), (0, 8 - H), (0, 0)))
    cot = jnp.swapaxes(cotangent[0], 0, 1).reshape(rows * width, channels)
    token = jnp.arange(width, dtype=jnp.int32)
    spread = ((token // rows) * block + (token % rows) * rows)[None, :]
    gather = ((token // rows) * block + token % rows)[:, None]
    size = rows * width
    shape = jax.ShapeDtypeStruct
    vmem = pltpu.VMEM
    whole = pl.BlockSpec(memory_space=pltpu.VMEM)
    out, grad, gproj, gout, tail = pl.pallas_call(
        functools.partial(kernel, n, rows, width, small, block, chunk),
        out_shape=(
            shape((size, channels), BF16),
            shape((size, channels), BF16),
            shape((2, channels, 4 * channels), F32),
            shape((2, channels, channels), F32),
            shape((2, 32, channels), F32),
        ),
        in_specs=[whole] * 9,
        out_specs=(whole,) * 5,
        scratch_shapes=[
            vmem((2, size, channels), F32),
            vmem((2, size, channels), F32),
            vmem((2, size, channels), BF16),
            vmem((2, size, 4 * channels), BF16),
            vmem((2, size, channels), F32),
            vmem((2, size, channels), F32),
            vmem((size, channels), F32),
            vmem((2, size, channels), BF16),
            vmem((size, 4 * channels), BF16),
            vmem((size, channels), BF16),
            vmem((size, channels), BF16),
            vmem((2, H * width, width), F32),
            vmem((H * width, width), F32),
            vmem((rows, H * width, width) if small else (1, 8, 128), F32),
            vmem((slots, width, 8, width), F32),
            vmem((slots, width, 8, width), F32),
            vmem((slots, n, rows, 8, width), F32),
            vmem((slots, n, block, channels), BF16),
            vmem((slots, n, block, channels), BF16),
            vmem((2, 2 * n * chunk, channels), F32),
            vmem((2, n * chunk, channels), F32),
            vmem((2, n, chunk, channels), F32),
            vmem((2, n, chunk, channels), F32),
            vmem((2, 2, n, chunk, channels), F32),
            vmem((n, 32, channels), F32),
            pltpu.SemaphoreType.DMA((11, n)),
            pltpu.SemaphoreType.DMA((11, n)),
            pltpu.SemaphoreType.DMA((5,)),
            pltpu.SemaphoreType.DMA((5,)),
        ],
        compiler_params=pltpu.CompilerParams(
            collective_id=0, has_side_effects=True, vmem_limit_bytes=(40 if small else 60) * 2**20
        ),
    )(pair.reshape(size, channels), pair_mask[0], ln_gain, projection_weight, wbias, w_out, cot, spread, gather)
    pair_out = jnp.swapaxes(out.reshape(rows, width, channels), 0, 1)[None]
    tail = tail[0].reshape(2, 16, channels)
    return (
        pair_out,
        grad.reshape(pair.shape),
        tail[:, 8],
        gproj,
        jnp.swapaxes(tail[:, :H], 1, 2),
        gout,
    )


def solution(mesh):
    placed = (
        P(("groups", "dp"), "axial", None, None),
        P(("groups", "dp"), "axial", None),
        P(),
        P(),
        P(),
        P(),
        P(("groups", "dp"), None, "axial", None),
    )
    return jax.shard_map(
        functools.partial(local, mesh.shape["axial"]),
        mesh=mesh,
        in_specs=placed,
        out_specs=(
            P(("groups", "dp"), None, "axial", None),
            P(("groups", "dp"), "axial", None, None),
            P("groups", None),
            P("groups", None, None),
            P("groups", None, None),
            P("groups", None, None),
        ),
        check_vma=False,
    )
```

time: 406 us -> 70.2 us (0.17)
  blocking collectives: 162 us -> 0 us
  waiting for transfers between devices: 98.9 us -> 0 us
  matrix products: 67 us -> 0 us
  Pallas kernels: 0 us -> 59.7 us
  local copies, waits for them, and re-layouts: 38.5 us -> 9.43 us
  between operations: 15.2 us -> 0.67 us
  other arithmetic: 11.4 us -> 0.03 us
  starting transfers between devices: 9 us -> 0 us
    psum x1 -> x0, waiting for transfers between devices: 87.4 us -> none  [local(): lax.psum((grads_first[0], grads_first[1], grads_first[2], grads_first[3],...]
    unnamed x2 -> x0, blocking collectives: 69.4 us -> none
    all_gather x2 -> x0, blocking collectives: 62.9 us -> none  [attend_forward(): lax.all_gather(local_bias(normed_input, pair_bias_weight, column_view), '...]
    pallas_call x0 -> x1, Pallas kernels: none -> 59.7 us  [local(): pl.pallas_call(functools.partial(kernel, n, rows, width, small, block, ch...]
    dot_general x102 -> x0, matrix products: 53.6 us -> none  [the longest x24 24.8 us: one_row(): jnp.einsum('nhbk,nkhd->nbhd', probs_b, values, preferred_element_type=jnp...]
    psum x1 -> x0, blocking collectives: 30 us -> none  [local(): lax.psum((grads_first[0], grads_first[1], grads_first[2], grads_first[3],...]
    broadcast_in_dim x24 -> x0, local copies, waits for them, and re-layouts: 14.7 us -> none  [the longest x12 10.8 us: one_row(): jnp.where(keep_row[:, None, None, :], probs * (d_probs - total), 0.0)]
    sub x24 -> x0, matrix products: 13.4 us -> none  [row_probs(): probs = jax.nn.softmax(scores, axis=-1)]
  transfers between devices with their start and end apart: 3 -> 0, of which waited for: 3 -> 0; matrix products, arithmetic and copies ran while one was open for 1% -> 0% of each run, Pallas kernels for 0% -> 0%
where the time goes in v1:
time: 70.2 us; the launch traced here: 69.9 us
  Pallas kernels  59.7 us (85%)
  local copies, waits for them, and re-layouts  9.43 us (13%)
    pallas_call x1, Pallas kernels, local(): pl.pallas_call(functools.partial(kernel, n, rows, width, small, block, ch...  59.7 us
    unnamed x19, local copies, waits for them, and re-layouts  8.27 us

profile of v1, /device:TPU:0, one launch (start us, length us, event | category | flops | bytes accessed | tf_op | source)
XLA Modules:
  0.0 69.9 jit_solution(5961293892619128118)
XLA Ops:
  0.6 0.0 copy-start.5
  0.7 0.7 copy-done.5
  1.3 0.0 copy-start.6
  1.3 0.7 copy-done.6
  2.0 0.0 copy-start.4
  2.0 0.7 copy-done.4
  2.7 0.0 copy-start
  2.7 0.9 %copy-done = bf16[2,128,512]{2,1,0:T(8,128)(2,1)S(1)} copy-done((bf16[2,128,512]{2,1,0:T(8,128)(2,1)S(1)}, bf16[2,128,512]{2,1,0:T(8,128)(2,1)}, u32[]{:S(2)}) %copy-start) | copy-done | bytes 262168
  3.6 0.0 copy-start.1
  3.6 0.9 %copy-done.1 = bf16[1,6,48,128]{3,2,1,0:T(8,128)(2,1)S(1)} copy-done((bf16[1,6,48,128]{3,2,1,0:T(8,128)(2,1)S(1)}, bf16[1,6,48,128]{3,2,1,0:T(8,128)(2,1)}, u32[]{:S(2)}) %copy-start.1) | copy-done | bytes 73752
  4.5 0.0 copy-start.2
  4.5 0.9 %copy-done.2 = bf16[1,48,6,128]{3,1,2,0:T(8,128)(2,1)S(1)} copy-done((bf16[1,48,6,128]{3,1,2,0:T(8,128)(2,1)S(1)}, bf16[1,48,6,128]{3,1,2,0:T(8,128)(2,1)}, u32[]{:S(2)}) %copy-start.2) | copy-done | bytes 73752
  5.4 0.0 copy-start.3
  5.4 0.8 %copy-done.3 = bf16[2,128,128]{2,1,0:T(8,128)(2,1)S(1)} copy-done((bf16[2,128,128]{2,1,0:T(8,128)(2,1)S(1)}, bf16[2,128,128]{2,1,0:T(8,128)(2,1)}, u32[]{:S(2)}) %copy-start.3) | copy-done | bytes 65560
  6.2 59.7 %shard_map.118 = (bf16[288,128]{1,0:T(8,128)(2,1)S(1)}, bf16[288,128]{1,0:T(8,128)(2,1)S(1)}, f32[2,128,512]{2,1,0:T(8,128)S(1)}, f32[2,128,128]{2,1,0:T(8,128)S(1)}, f32[2,32,128]{2,1,0:T(8,128)S(1)}) custom-call(bf16[288,128]{1,0:T(8,128)(2,1)S(1)} %bitcast.20, s32[6,48]{1,0:T(8,128)S(1)} %bitcast.24, f32[2,128]{1,0:T(2,128)S(1)} %copy-done.4, ...), custom_call_target="tpu_custom_call" | custom-call | tf_op jit(solution)/shard_map/pallas_call | solution.py:372
  66.0 0.6 slice.12
  66.6 0.6 slice_bitcast_fusion
  67.2 0.6 copy.20
  67.8 0.6 copy.21
  68.4 0.8 %copy.22 = f32[2,128,512]{2,1,0:T(8,128)} copy(f32[2,128,512]{2,1,0:T(8,128)S(1)} %get-tuple-element.25) | data formatting | bytes 1048576
  69.2 0.7 copy.23
  (5 shorter events, 0.0 us)
Async XLA Ops:
  0.6 0.7 copy-start.5
  1.3 0.7 copy-start.6
  2.0 0.7 copy-start.4
  2.7 0.9 %copy-start = (bf16[2,128,512]{2,1,0:T(8,128)(2,1)S(1)}, bf16[2,128,512]{2,1,0:T(8,128)(2,1)}, u32[]{:S(2)}) copy-start(bf16[2,128,512]{2,1,0:T(8,128)(2,1)} %wproj_ref.1) | copy-start | bytes 786436
  3.6 0.9 %copy-start.1 = (bf16[1,6,48,128]{3,2,1,0:T(8,128)(2,1)S(1)}, bf16[1,6,48,128]{3,2,1,0:T(8,128)(2,1)}, u32[]{:S(2)}) copy-start(bf16[1,6,48,128]{3,2,1,0:T(8,128)(2,1)} %param.7) | copy-start | bytes 221188
  4.5 0.9 %copy-start.2 = (bf16[1,48,6,128]{3,1,2,0:T(8,128)(2,1)S(1)}, bf16[1,48,6,128]{3,1,2,0:T(8,128)(2,1)}, u32[]{:S(2)}) copy-start(bf16[1,48,6,128]{3,1,2,0:T(8,128)(2,1)} %param.13) | copy-start | bytes 221188
  5.4 0.8 %copy-start.3 = (bf16[2,128,128]{2,1,0:T(8,128)(2,1)S(1)}, bf16[2,128,128]{2,1,0:T(8,128)(2,1)}, u32[]{:S(2)}) copy-start(bf16[2,128,128]{2,1,0:T(8,128)(2,1)} %wout_ref.1) | copy-start | bytes 196612

commit v2 on v1

--- a/solution.py
+++ b/solution.py
@@ -22,11 +22,12 @@
 
 def kernel(
     n, rows, width, small, block, chunk,
-    pair_ref, mask_ref, gain_ref, wproj_ref, wbias_ref, wout_ref, cot_ref, spread_ref, gather_ref,
-    out_ref, grad_ref, gproj_ref, gout_ref, tail_ref,
+    pair_in, mask_in, gain_in, wproj_in, wbias_in, wout_in, cot_in,
+    out_hbm, grad_hbm, gproj_hbm, gout_hbm, gbias_ref, ggain_ref,
+    pair_ref, mask_ref, gain_ref, wproj_ref, wbias_raw, wbias_ref, wout_ref, cot_ref, out_ref, grad_ref, tail_ref,
     xhat, rstd, normed, proj, gate, att, dgated, gated, dproj, x2, dy1, bias, dacc, kept,
     bgat, dsend, drecv, asend, arecv, part, fromcore, half, red, full, tails,
-    send_sem, recv_sem, core_send, core_recv,
+    send_sem, recv_sem, core_send, core_recv, in_sem, out_sem,
 ):
     me = lax.axis_index("axial")
     core = lax.axis_index("dp")
@@ -36,6 +37,7 @@
     scale = 1.0 / math.sqrt(head)
     stack = H if small else 1
     half_rows = n * chunk
+    tight = width <= 64 and rows <= 8
 
     def slot_of(l):
         return l if small else 0
@@ -46,6 +48,16 @@
                 body(idx)
         else:
             lax.fori_loop(low, high, lambda idx, c: (body(idx), c)[1], 0)
+
+    loads = [
+        pltpu.make_async_copy(source, target, in_sem.at[idx])
+        for idx, (source, target) in enumerate((
+            (pair_in, pair_ref), (gain_in, gain_ref), (wbias_in, wbias_raw), (wproj_in, wproj_ref),
+            (mask_in, mask_ref), (wout_in, wout_ref), (cot_in, cot_ref),
+        ))
+    ]
+    for load in loads:
+        load.start()
 
     barrier = pltpu.get_barrier_semaphore()
 
@@ -78,8 +90,22 @@
     def at_row(a):
         return pl.ds(a * width if small else pl.multiple_of(a * width, 16), width)
 
+    def place(token, step):
+        peer = ((token.astype(F32) + 0.5) * (1.0 / rows)).astype(jnp.int32)
+        return peer * block + (token - peer * rows) * step
+
+    spread = place(lax.broadcasted_iota(jnp.int32, (1, width), 1), rows)
+    gather = place(lax.broadcasted_iota(jnp.int32, (width, 1), 0), 1)
+
     lanes = lax.broadcasted_iota(jnp.int32, (1, channels), 1)
     head_masks = [jnp.where((lanes >= h * head) & (lanes < (h + 1) * head), 1.0, 0.0) for h in range(H)]
+
+    def packing(axis):
+        shape = (width, n * 8) if axis == 0 else (n * 8, width)
+        token = lax.broadcasted_iota(jnp.int32, (width, 1) if axis == 0 else (1, width), axis)
+        peer = ((token.astype(F32) + 0.5) * (1.0 / rows)).astype(jnp.int32)
+        spots = lax.broadcasted_iota(jnp.int32, shape, 1 - axis)
+        return jnp.where(spots == token + peer * (8 - rows), 1.0, 0.0)
 
     def stacked(value, first):
         value = value.astype(F32)
@@ -101,7 +127,13 @@
         normed[l] = (hat * gain_ref[l : l + 1]).astype(BF16)
 
         def own_bias(a):
-            bgat[slot_of(l), me * rows + a] = dot(wbias_ref[l], normed[l, at_row(a)], 1, 1)
+            values = dot(wbias_ref[l], normed[l, at_row(a)], 1, 1)
+            if tight:
+                for h in range(H):
+                    low = (h % 2) * 64
+                    bgat[l, me, h // 2, a : a + 1, low : low + width] = values[h : h + 1]
+            else:
+                bgat[slot_of(l), me * rows + a] = values
 
         steps(0, rows, own_bias)
 
@@ -111,18 +143,26 @@
         gate[l] = jax.nn.sigmoid(values[:, 3 * channels :].astype(F32))
 
     def bias_source(l):
-        return lambda peer: bgat.at[slot_of(l), pl.ds(me * rows, rows)]
+        return lambda peer: bgat.at[l, me] if tight else bgat.at[slot_of(l), pl.ds(me * rows, rows)]
 
     def bias_target(l):
-        return lambda slot: bgat.at[slot_of(l), pl.ds(slot * rows, rows)]
+        return lambda slot: bgat.at[l, slot] if tight else bgat.at[slot_of(l), pl.ds(slot * rows, rows)]
 
     def stack_bias(l):
+        if tight:
+            chosen = packing(0)
+            for pair in range(H // 2):
+                values = dot(chosen, bgat[l, :, pair].reshape(n * 8, 128), 1, 0, HIGHEST)
+                for u in range(2):
+                    first = (2 * pair + u) * width
+                    bias[l, first : first + width] = values[:, u * 64 : u * 64 + width]
+            return
         for h in range(H):
             bias[l, h * width : (h + 1) * width] = bgat[slot_of(l), :, h, :]
 
     def probabilities(l, a, first, queries, keys):
         scores = dot(queries, keys, 1, 1) * scale + bias[l, first * width : (first + stack) * width]
-        scores = jnp.where(mask_ref[pl.ds(a, 1)] > 0, scores, MASKED)
+        scores = jnp.where(mask_ref[a] > 0, scores, MASKED)
         top = jnp.max(scores, axis=-1, keepdims=True)
         weights = jnp.exp(scores - top)
         return weights * (1.0 / jnp.sum(weights, axis=-1, keepdims=True))
@@ -146,7 +186,7 @@
         gates = gate[l, at_row(a)]
         d_row = dgated[at_row(a)]
         d_att = (d_row * gates).astype(BF16)
-        keep = mask_ref[pl.ds(a, 1)] > 0
+        keep = mask_ref[a] > 0
         total = d_query = d_keys = d_values = None
         for first in range(0, H, stack):
             queries = stacked(query, first)
@@ -190,7 +230,7 @@
             total = None
             for a in range(rows):
                 spots = lax.broadcasted_iota(jnp.int32, (length, width), 0) + (base - a)
-                chosen = jnp.where(spots == spread_ref[...], 1.0, 0.0).astype(BF16)
+                chosen = jnp.where(spots == spread, 1.0, 0.0).astype(BF16)
                 term = dot(chosen, value_at(a), 1, 0)
                 total = term if total is None else total + term
             return total.astype(BF16)
@@ -211,21 +251,31 @@
 
         def one(a):
             spots = lax.broadcasted_iota(jnp.int32, (width, n * block), 1) - a * rows
-            chosen = jnp.where(spots == gather_ref[...], 1.0, 0.0).astype(BF16)
+            chosen = jnp.where(spots == gather, 1.0, 0.0).astype(BF16)
             target[at_row(a)] = dot(chosen, arrived, 1, 0).astype(BF16)
 
         steps(0, rows, one)
 
     def ds_source(l):
-        return lambda peer: dsend.at[slot_of(l), pl.ds(peer * rows, rows)]
+        return lambda peer: dsend.at[l, peer] if tight else dsend.at[slot_of(l), pl.ds(peer * rows, rows)]
 
     def ds_target(l):
         return lambda slot: drecv.at[slot_of(l), slot]
 
     def send_bias_grad(l):
-        for h in range(H):
-            dsend[slot_of(l), :, h, :] = dacc[h * width : (h + 1) * width]
-        drecv[slot_of(l), me] = dsend[slot_of(l), pl.ds(me * rows, rows)]
+        if tight:
+            chosen = packing(1)
+            gap = jnp.zeros((width, 64 - width), F32)
+            for pair in range(H // 2):
+                first = 2 * pair * width
+                both = [dacc[first : first + width], gap, dacc[first + width : first + 2 * width], gap]
+                values = dot(chosen, jnp.concatenate(both, axis=1), 1, 0, HIGHEST)
+                dsend[l, :, pair] = values.reshape(n, 8, 128)
+            drecv[l, me] = dsend[l, me]
+        else:
+            for h in range(H):
+                dsend[slot_of(l), :, h, :] = dacc[h * width : (h + 1) * width]
+            drecv[slot_of(l), me] = dsend[slot_of(l), pl.ds(me * rows, rows)]
         start(2 + l, ds_source(l), ds_target(l))
 
     def weight_grads(l, dy):
@@ -251,25 +301,39 @@
         start(6 + l, reduce_source(l), reduce_target(l))
 
     def full_source(l):
-        return lambda peer: full.at[l, core, me]
+        return lambda peer: full.at[l, chunk_at(me)]
 
     def full_target(l):
-        return lambda slot: full.at[l, core, slot]
+        return lambda slot: full.at[l, chunk_at(slot)]
+
+    def chunk_at(slot):
+        return pl.ds(pl.multiple_of((core * n + slot) * chunk, 8), chunk)
+
+    def half_at(which):
+        return pl.ds(pl.multiple_of(which * half_rows, 8), half_rows)
 
     def axial_sum(l):
         finish(6 + l, reduce_source(l), reduce_target(l))
-        full[l, core, me] = jnp.sum(red[l], axis=0)
+        full[l, chunk_at(me)] = jnp.sum(red[l], axis=0)
         start(8 + l, full_source(l), full_target(l))
 
     def core_last(l):
-        return core_copy(2 + l, full.at[l, core], full.at[l, core])
+        return core_copy(2 + l, full.at[l, half_at(core)], full.at[l, half_at(core)])
 
     def core_last_wait(l):
-        return core_copy(2 + l, full.at[l, core], full.at[l, other])
+        return core_copy(2 + l, full.at[l, half_at(core)], full.at[l, half_at(other)])
 
     def layer_norm_grad(l, dn, dy):
         finish(2 + l, ds_source(l), ds_target(l))
         own = jnp.sum(drecv[slot_of(l)], axis=0)
+        if tight:
+            spare = jnp.zeros((8 - H, width), F32)
+            own = [
+                jnp.concatenate(
+                    [own[h // 2, a : a + 1, (h % 2) * 64 : (h % 2) * 64 + width] for h in range(H)] + [spare], axis=0
+                )
+                for a in range(rows)
+            ]
         extra, bias_grad = [], None
         weights = wbias_ref[l].astype(F32)
         for a in range(rows):
@@ -285,20 +349,37 @@
             - jnp.mean(d_hat, axis=-1, keepdims=True)
             - hat * jnp.mean(d_hat * hat, axis=-1, keepdims=True)
         )
-        tails[me, l * 16 : l * 16 + 8] = bias_grad
-        tails[me, l * 16 + 8 : l * 16 + 16] = jnp.broadcast_to(gain_grad, (8, channels))
+        tails[me, l * 8 : l * 8 + H] = bias_grad[:H]
+        tails[me, l * 8 + H : l * 8 + 8] = jnp.broadcast_to(gain_grad, (8 - H, channels))
         return (dy.astype(F32) + rstd[l] * inner).astype(BF16)
 
-    dsend[...] = jnp.zeros(dsend.shape, F32)
+    stores = []
+
+    def store(idx, source, target):
+        stores.append(pltpu.make_async_copy(source, target, out_sem.at[idx]))
+        stores[-1].start()
+
+    if tight:
+        bgat[:, me] = jnp.zeros((2,) + bgat.shape[2:], F32)
+    else:
+        dsend[...] = jnp.zeros(dsend.shape, F32)
     if half_rows * 2 > 5 * channels:
         part[...] = jnp.zeros(part.shape, F32)
 
+    for load in loads[:3]:
+        load.wait()
+    for l in range(2):
+        spare = jnp.zeros((8 - H, channels), F32)
+        wbias_ref[l] = jnp.concatenate([wbias_raw[l].astype(F32), spare], axis=0).astype(BF16)
     prepare(0, pair_ref)
     pl.semaphore_wait(barrier, n)
     start(0, bias_source(0), bias_target(0))
+    loads[3].wait()
     project(0)
     finish(0, bias_source(0), bias_target(0))
     stack_bias(0)
+    for load in loads[4:]:
+        load.wait()
     steps(0, rows, forward_row)
     asend_value = gate_output(0, pair_ref)
     turn_send(0, lambda a: asend_value[a * width : (a + 1) * width])
@@ -315,6 +396,7 @@
     steps(0, rows, functools.partial(backward_row, 1))
     send_bias_grad(1)
     out_ref[...] = gate_output(1, x2)
+    store(0, out_ref, out_hbm)
     dn = dot(dproj[...], wproj_ref[1], 1, 1)
     weight_grads(1, cot_ref[...])
     core_first(1).start()
@@ -334,6 +416,7 @@
     dn = dot(dproj[...], wproj_ref[0], 1, 1)
     core_sum(0)
     grad_ref[...] = layer_norm_grad(0, dn, dy1[...])
+    store(1, grad_ref, grad_hbm)
     start(10, lambda peer: tails.at[me], lambda slot: tails.at[slot])
     axial_sum(0)
     finish(8 + 1, full_source(1), full_target(1))
@@ -346,41 +429,68 @@
     core_last(0).start()
     core_copy(4, tail_ref.at[0], tail_ref.at[1]).wait()
     tail_ref[0] = tail_ref[0] + tail_ref[1]
+    for l in range(2):
+        gbias_ref[l] = tail_ref[0, l * 8 : l * 8 + H]
+        ggain_ref[l : l + 1] = tail_ref[0, l * 8 + H : l * 8 + H + 1]
     for l in (1, 0):
         core_last_wait(l).wait()
-        values = full[l].reshape(2 * half_rows, channels)
         for e in range(4):
-            gproj_ref[l, :, e * channels : (e + 1) * channels] = values[e * channels : (e + 1) * channels]
-        gout_ref[l] = values[4 * channels : 5 * channels]
+            store(
+                2 + 5 * l + e, full.at[l, pl.ds(e * channels, channels)],
+                gproj_hbm.at[l, :, pl.ds(e * channels, channels)],
+            )
+        store(6 + 5 * l, full.at[l, pl.ds(4 * channels, channels)], gout_hbm.at[l])
+    for copy in stores:
+        copy.wait()
+
+
+def hand_over(*refs):
+    copies = [pltpu.make_async_copy(refs[idx], refs[6 + idx], refs[12].at[idx]) for idx in range(6)]
+    for copy in copies:
+        copy.start()
+    for copy in copies:
+        copy.wait()
 
 
 def local(n, pair, pair_mask, ln_gain, projection_weight, pair_bias_weight, w_out, cotangent):
     rows, width, channels = pair.shape[1:]
     small = width <= 128
     slots = 2 if small else 1
+    tight = width <= 64 and rows <= 8
     block = -(-rows * rows // 16) * 16
     chunk = -(-5 * channels // (2 * n * 8)) * 8
-    wbias = jnp.pad(jnp.swapaxes(pair_bias_weight, 1, 2), ((0, 0), (0, 8 - H), (0, 0)))
+    wbias = jnp.swapaxes(pair_bias_weight, 1, 2)
     cot = jnp.swapaxes(cotangent[0], 0, 1).reshape(rows * width, channels)
-    token = jnp.arange(width, dtype=jnp.int32)
-    spread = ((token // rows) * block + (token % rows) * rows)[None, :]
-    gather = ((token // rows) * block + token % rows)[:, None]
     size = rows * width
     shape = jax.ShapeDtypeStruct
     vmem = pltpu.VMEM
     whole = pl.BlockSpec(memory_space=pltpu.VMEM)
-    out, grad, gproj, gout, tail = pl.pallas_call(
+    hbm = pl.BlockSpec(memory_space=pltpu.HBM)
+    results = (
+        shape((size, channels), BF16),
+        shape((size, channels), BF16),
+        shape((2, channels, 4 * channels), F32),
+        shape((2, channels, channels), F32),
+        shape((2, H, channels), F32),
+        shape((2, channels), F32),
+    )
+    made = pl.pallas_call(
         functools.partial(kernel, n, rows, width, small, block, chunk),
-        out_shape=(
-            shape((size, channels), BF16),
-            shape((size, channels), BF16),
-            shape((2, channels, 4 * channels), F32),
-            shape((2, channels, channels), F32),
-            shape((2, 32, channels), F32),
-        ),
-        in_specs=[whole] * 9,
-        out_specs=(whole,) * 5,
+        out_shape=results,
+        in_specs=[hbm] * 7,
+        out_specs=(hbm,) * 4 + (whole,) * 2,
         scratch_shapes=[
+            vmem((size, channels), BF16),
+            vmem((rows, 1, width), jnp.int32),
+            vmem((2, channels), F32),
+            vmem((2, channels, 4 * channels), BF16),
+            vmem((2, H, channels), BF16),
+            vmem((2, 8, channels), BF16),
+            vmem((2, channels, channels), BF16),
+            vmem((size, channels), BF16),
+            vmem((size, channels), BF16),
+            vmem((size, channels), BF16),
+            vmem((2, 16, channels), F32),
             vmem((2, size, channels), F32),
             vmem((2, size, channels), F32),
             vmem((2, size, channels), BF16),
@@ -395,34 +505,42 @@
             vmem((2, H * width, width), F32),
             vmem((H * width, width), F32),
             vmem((rows, H * width, width) if small else (1, 8, 128), F32),
-            vmem((slots, width, 8, width), F32),
-            vmem((slots, width, 8, width), F32),
-            vmem((slots, n, rows, 8, width), F32),
+            vmem((2, n, 2, 8, 128) if tight else (slots, width, 8, width), F32),
+            vmem((2, n, 2, 8, 128) if tight else (slots, width, 8, width), F32),
+            vmem((2, n, 2, 8, 128) if tight else (slots, n, rows, 8, width), F32),
             vmem((slots, n, block, channels), BF16),
             vmem((slots, n, block, channels), BF16),
             vmem((2, 2 * n * chunk, channels), F32),
             vmem((2, n * chunk, channels), F32),
             vmem((2, n, chunk, channels), F32),
             vmem((2, n, chunk, channels), F32),
-            vmem((2, 2, n, chunk, channels), F32),
-            vmem((n, 32, channels), F32),
+            vmem((2, 2 * n * chunk, channels), F32),
+            vmem((n, 16, channels), F32),
             pltpu.SemaphoreType.DMA((11, n)),
             pltpu.SemaphoreType.DMA((11, n)),
             pltpu.SemaphoreType.DMA((5,)),
             pltpu.SemaphoreType.DMA((5,)),
+            pltpu.SemaphoreType.DMA((7,)),
+            pltpu.SemaphoreType.DMA((12,)),
         ],
         compiler_params=pltpu.CompilerParams(
-            collective_id=0, has_side_effects=True, vmem_limit_bytes=(40 if small else 60) * 2**20
+            collective_id=0, has_side_effects=True, vmem_limit_bytes=63 * 2**20
         ),
-    )(pair.reshape(size, channels), pair_mask[0], ln_gain, projection_weight, wbias, w_out, cot, spread, gather)
-    pair_out = jnp.swapaxes(out.reshape(rows, width, channels), 0, 1)[None]
-    tail = tail[0].reshape(2, 16, channels)
+    )(pair.reshape(size, channels), pair_mask.reshape(rows, 1, width), ln_gain, projection_weight, wbias, w_out, cot)
+    out, grad, gproj, gout, gbias, ggain = pl.pallas_call(
+        hand_over,
+        out_shape=results,
+        in_specs=[hbm] * 6,
+        out_specs=(hbm,) * 6,
+        scratch_shapes=[pltpu.SemaphoreType.DMA((6,))],
+        compiler_params=pltpu.CompilerParams(vmem_limit_bytes=63 * 2**20),
+    )(*made)
     return (
-        pair_out,
+        jnp.swapaxes(out.reshape(rows, width, channels), 0, 1)[None],
         grad.reshape(pair.shape),
-        tail[:, 8],
+        ggain,
         gproj,
-        jnp.swapaxes(tail[:, :H], 1, 2),
+        jnp.swapaxes(gbias, 1, 2),
         gout,
     )
 

time: 70.2 us -> 81.4 us (1.16)
  Pallas kernels: 59.7 us -> 80.6 us
  local copies, waits for them, and re-layouts: 9.43 us -> 0 us
    pallas_call x0 -> x1, Pallas kernels: none -> 25.6 us  [local(): pl.pallas_call(hand_over, out_shape=results, in_specs=[hbm] * 6, out_spec...]
    unnamed x19 -> x0, local copies, waits for them, and re-layouts: 8.27 us -> none
    pallas_call x1, Pallas kernels: 59.7 us -> 55 us  [local(): pl.pallas_call(functools.partial(kernel, n, rows, width, small, block, ch...]
where the time goes in v2:
time: 81.4 us; the launch traced here: 81.3 us
  Pallas kernels  80.6 us (99%)
    pallas_call x1, Pallas kernels, local(): pl.pallas_call(functools.partial(kernel, n, rows, width, small, block, ch...  55 us
    pallas_call x1, Pallas kernels, local(): pl.pallas_call(hand_over, out_shape=results, in_specs=[hbm] * 6, out_spec...  25.6 us

profile of v2, /device:TPU:0, one launch (start us, length us, event | category | flops | bytes accessed | tf_op | source)
XLA Modules:
  0.0 81.3 jit_solution(8214219183662051812)
XLA Ops:
  0.6 55.0 %shard_map.118 = (bf16[288,128]{1,0:T(8,128)(2,1)}, bf16[288,128]{1,0:T(8,128)(2,1)}, f32[2,128,512]{2,1,0:T(8,128)}, f32[2,128,128]{2,1,0:T(8,128)}, f32[2,4,128]{2,1,0:T(4,128)}, /*index=5*/f32[2,128]{1,0:T(2,128)}) custom-call(bf16[288,128]{1,0:T(8,128)(2,1)} %bitcast.15, s32[6,1,48]{2,1,0:T(1,128)} %bitcast.17, f32[2,128]{1,0:T(2,128)} %gain_in.1, ...), custom_call_target="tpu_custom_call" | custom-call | tf_op jit(solution)/shard_map/pallas_call | solution.py:477
  55.6 25.6 %shard_map.119 = (bf16[288,128]{1,0:T(8,128)(2,1)}, bf16[288,128]{1,0:T(8,128)(2,1)}, f32[2,128,512]{2,1,0:T(8,128)}, f32[2,128,128]{2,1,0:T(8,128)}, f32[2,4,128]{2,1,0:T(4,128)}, /*index=5*/f32[2,128]{1,0:T(2,128)}) custom-call(bf16[288,128]{1,0:T(8,128)(2,1)} %get-tuple-element.18.refs_0_, bf16[288,128]{1,0:T(8,128)(2,1)} %get-tuple-element.19.refs_1_, ...), custom_call_target="tpu_custom_call" | custom-call | tf_op jit(solution)/shard_map/pallas_call | solution.py:530

commit v3 on v2

--- a/solution.py
+++ b/solution.py
@@ -408,9 +408,10 @@
     dgated[...] = dot(dy1[...], wout_ref[0], 1, 1)
     if not small:
         dacc[...] = jnp.zeros(dacc.shape, F32)
-    steps(0, rows, functools.partial(backward_row, 0))
+    steps(0, rows // 2, functools.partial(backward_row, 0))
+    axial_sum(1)
+    steps(rows // 2, rows, functools.partial(backward_row, 0))
     send_bias_grad(0)
-    axial_sum(1)
     weight_grads(0, dy1[...])
     core_first(0).start()
     dn = dot(dproj[...], wproj_ref[0], 1, 1)
@@ -445,10 +446,15 @@
 
 
 def hand_over(*refs):
-    copies = [pltpu.make_async_copy(refs[idx], refs[6 + idx], refs[12].at[idx]) for idx in range(6)]
-    for copy in copies:
+    sources, targets, held, semaphore = refs[:6], refs[6:12], refs[12:18], refs[18]
+    inward = [pltpu.make_async_copy(sources[idx], held[idx], semaphore.at[0, idx]) for idx in range(6)]
+    outward = [pltpu.make_async_copy(held[idx], targets[idx], semaphore.at[1, idx]) for idx in range(6)]
+    for copy in inward:
         copy.start()
-    for copy in copies:
+    for idx in range(6):
+        inward[idx].wait()
+        outward[idx].start()
+    for copy in outward:
         copy.wait()
 
 
@@ -532,7 +538,7 @@
         out_shape=results,
         in_specs=[hbm] * 6,
         out_specs=(hbm,) * 6,
-        scratch_shapes=[pltpu.SemaphoreType.DMA((6,))],
+        scratch_shapes=[vmem(item.shape, item.dtype) for item in results] + [pltpu.SemaphoreType.DMA((2, 6))],
         compiler_params=pltpu.CompilerParams(vmem_limit_bytes=63 * 2**20),
     )(*made)
     return (

time: 81.4 us -> 58.6 us (0.72)
  Pallas kernels: 80.6 us -> 57.8 us
    pallas_call x1, Pallas kernels: 25.6 us -> 2.06 us  [local(): pl.pallas_call(hand_over, out_shape=results, in_specs=[hbm] * 6, out_spec...]
where the time goes in v3:
time: 58.6 us; the launch traced here: 58.5 us
  Pallas kernels  57.8 us (99%)
  between operations  0.64 us (1%)
    pallas_call x1, Pallas kernels, local(): pl.pallas_call(functools.partial(kernel, n, rows, width, small, block, ch...  55.8 us
    pallas_call x1, Pallas kernels, local(): pl.pallas_call(hand_over, out_shape=results, in_specs=[hbm] * 6, out_spec...  2.06 us

profile of v3, /device:TPU:0, one launch (start us, length us, event | category | flops | bytes accessed | tf_op | source)
XLA Modules:
  0.0 58.5 jit_solution(16774844103655707627)
XLA Ops:
  0.6 55.8 %shard_map.118 = (bf16[288,128]{1,0:T(8,128)(2,1)}, bf16[288,128]{1,0:T(8,128)(2,1)}, f32[2,128,512]{2,1,0:T(8,128)}, f32[2,128,128]{2,1,0:T(8,128)}, f32[2,4,128]{2,1,0:T(4,128)}, /*index=5*/f32[2,128]{1,0:T(2,128)}) custom-call(bf16[288,128]{1,0:T(8,128)(2,1)} %bitcast.15, s32[6,1,48]{2,1,0:T(1,128)} %bitcast.17, f32[2,128]{1,0:T(2,128)} %gain_in.1, ...), custom_call_target="tpu_custom_call" | custom-call | tf_op jit(solution)/shard_map/pallas_call | solution.py:483
  56.4 2.1 %shard_map.119 = (bf16[288,128]{1,0:T(8,128)(2,1)}, bf16[288,128]{1,0:T(8,128)(2,1)}, f32[2,128,512]{2,1,0:T(8,128)}, f32[2,128,128]{2,1,0:T(8,128)}, f32[2,4,128]{2,1,0:T(4,128)}, /*index=5*/f32[2,128]{1,0:T(2,128)}) custom-call(bf16[288,128]{1,0:T(8,128)(2,1)} %get-tuple-element.18.refs_0_, bf16[288,128]{1,0:T(8,128)(2,1)} %get-tuple-element.19.refs_1_, ...), custom_call_target="tpu_custom_call" | custom-call | tf_op jit(solution)/shard_map/pallas_call | solution.py:536

commit v4 on v3

--- a/solution.py
+++ b/solution.py
@@ -408,18 +408,17 @@
     dgated[...] = dot(dy1[...], wout_ref[0], 1, 1)
     if not small:
         dacc[...] = jnp.zeros(dacc.shape, F32)
-    steps(0, rows // 2, functools.partial(backward_row, 0))
+    steps(0, rows, functools.partial(backward_row, 0))
+    send_bias_grad(0)
     axial_sum(1)
-    steps(rows // 2, rows, functools.partial(backward_row, 0))
-    send_bias_grad(0)
     weight_grads(0, dy1[...])
     core_first(0).start()
     dn = dot(dproj[...], wproj_ref[0], 1, 1)
     core_sum(0)
+    axial_sum(0)
     grad_ref[...] = layer_norm_grad(0, dn, dy1[...])
     store(1, grad_ref, grad_hbm)
     start(10, lambda peer: tails.at[me], lambda slot: tails.at[slot])
-    axial_sum(0)
     finish(8 + 1, full_source(1), full_target(1))
     core_last(1).start()
     finish(10, lambda peer: tails.at[me], lambda slot: tails.at[slot])

time: 58.6 us -> 58.9 us (level)
  no operation moved by 1% of the time
where the time goes in v4:
time: 58.9 us; the launch traced here: 58.7 us
  Pallas kernels  58.1 us (99%)
  between operations  0.64 us (1%)
    pallas_call x1, Pallas kernels, local(): pl.pallas_call(functools.partial(kernel, n, rows, width, small, block, ch...  56 us
    pallas_call x1, Pallas kernels, local(): pl.pallas_call(hand_over, out_shape=results, in_specs=[hbm] * 6, out_spec...  2.06 us

profile of v4, /device:TPU:0, one launch (start us, length us, event | category | flops | bytes accessed | tf_op | source)
XLA Modules:
  0.0 58.7 jit_solution(6040575150303711795)
XLA Ops:
  0.6 56.0 %shard_map.118 = (bf16[288,128]{1,0:T(8,128)(2,1)}, bf16[288,128]{1,0:T(8,128)(2,1)}, f32[2,128,512]{2,1,0:T(8,128)}, f32[2,128,128]{2,1,0:T(8,128)}, f32[2,4,128]{2,1,0:T(4,128)}, /*index=5*/f32[2,128]{1,0:T(2,128)}) custom-call(bf16[288,128]{1,0:T(8,128)(2,1)} %bitcast.15, s32[6,1,48]{2,1,0:T(1,128)} %bitcast.17, f32[2,128]{1,0:T(2,128)} %gain_in.1, ...), custom_call_target="tpu_custom_call" | custom-call | tf_op jit(solution)/shard_map/pallas_call | solution.py:482
  56.7 2.1 %shard_map.119 = (bf16[288,128]{1,0:T(8,128)(2,1)}, bf16[288,128]{1,0:T(8,128)(2,1)}, f32[2,128,512]{2,1,0:T(8,128)}, f32[2,128,128]{2,1,0:T(8,128)}, f32[2,4,128]{2,1,0:T(4,128)}, /*index=5*/f32[2,128]{1,0:T(2,128)}) custom-call(bf16[288,128]{1,0:T(8,128)(2,1)} %get-tuple-element.18.refs_0_, bf16[288,128]{1,0:T(8,128)(2,1)} %get-tuple-element.19.refs_1_, ...), custom_call_target="tpu_custom_call" | custom-call | tf_op jit(solution)/shard_map/pallas_call | solution.py:535
